TPU v7x, 512 devices: a whole 4x4x16 slice. The times are simulated.
512 devices in a mesh: row: 32 (over z, core), col: 16 (over y, x).
Axes of the slice: x: 4, y: 4, z: 16, core: 2. Of those that a mesh axis runs over, the one named last changes fastest.
Arguments:
- a_blocks: bfloat16 [32, 16, 96, 128, 128], P('row', 'col'), may hold values from -0.5 to 0.5
- a_rows: int32 [32, 16, 96], P('row', 'col'), may hold values from 0 to 31, as said below
- a_cols: int32 [32, 16, 96], P('row', 'col'), may hold values from 0 to 63, as said below
- p_blocks: bfloat16 [1024, 128, 256], P(('row', 'col')), may hold values from -0.5 to 0.5
- coarse_slot: int32 [32, 16, 96, 4, 4], P('row', 'col'), may hold values from 0 to 127
Outputs:
- coarse_blocks: bfloat16 [32, 128, 4096], P('row', 'col')
Inputs may be any that keep to these rules, and one draw needn't show every extreme that they name: On each owner the pairs (a_rows, a_cols) of its 96 blocks are distinct. On each owner the pairs (a_rows, a_cols) of its 96 blocks are distinct.
All inputs are finite; a program needn't handle non-finite values.
Results may differ from a plain program's by a relative error of at most 0.0049.
Values may be sent and summed in bfloat16 or wider, within the bound.
A program may use at most 128 MiB of HBM per device.

v0:
```python
import jax
import jax.numpy as jnp
from jax import lax
from jax.sharding import PartitionSpec as P

KS_DEV = 8


def copy_for_each(array, axis):
    size = lax.axis_size(axis)
    return lax.all_to_all(
        jnp.broadcast_to(array[None], (size, *array.shape)), axis, 0, 0, tiled=True
    )


def joined_along(tiles, dim):
    lengths = list(tiles.shape[1:])
    lengths[dim] *= tiles.shape[0]
    return jnp.moveaxis(tiles, 0, dim).reshape(lengths)


def collect(array, axis, dim):
    tiles = copy_for_each(array, axis)
    return joined_along(tiles, dim)


def in_blocks(array, dim, size):
    lengths = array.shape
    tiles = array.reshape(*lengths[:dim], size, lengths[dim] // size, *lengths[dim + 1 :])
    return jnp.moveaxis(tiles, dim, 0)


def sum_at_owner(array, axis, dim):
    tiles = in_blocks(array, dim, lax.axis_size(axis))
    arrived = lax.all_to_all(tiles, axis, split_axis=0, concat_axis=0, tiled=True)
    return arrived.sum(axis=0)


def owner_terms(blocks, row_ids, col_ids, slot_ids, row_panel, column_panel, slot_count):
    count = blocks.shape[0]
    group_size = 16
    groups = count // group_size
    node_width = blocks.shape[1]
    panel_width = row_panel.shape[2]
    agg_blocks = slot_ids.shape[1]
    agg_width = panel_width // agg_blocks

    def accumulate(running, batch_item):
        blk, rws, cls, sls = batch_item
        right_rows = jnp.take(column_panel, cls, axis=0)
        product = jnp.einsum(
            "kab,kbw->kaw", blk, right_rows, preferred_element_type=jnp.float32
        ).astype(jnp.bfloat16)
        left_rows = jnp.take(row_panel, rws, axis=0)
        left_split = left_rows.reshape(group_size, node_width, agg_blocks, agg_width)
        right_split = product.reshape(group_size, node_width, agg_blocks, agg_width)
        contribs = jnp.einsum(
            "knta,knsb->ktsab", left_split, right_split, preferred_element_type=jnp.float32
        )
        contribs = contribs.reshape(group_size * agg_blocks * agg_blocks, agg_width * agg_width)
        running = running.at[sls.reshape(-1)].add(contribs)
        return (running, None)

    items = (
        blocks.reshape(groups, group_size, node_width, node_width),
        row_ids.reshape(groups, group_size),
        col_ids.reshape(groups, group_size),
        slot_ids.reshape(groups, group_size, agg_blocks, agg_blocks),
    )
    start = jnp.zeros((slot_count, agg_width * agg_width), jnp.float32)
    running, _ = lax.scan(accumulate, start, items)
    return running


def on_device(a_blocks, a_rows, a_cols, p_blocks, coarse_slot):
    rows_total = lax.axis_size("row")
    cols_total = lax.axis_size("col")
    fan_count = rows_total // cols_total
    piece_rows = p_blocks.shape[0]
    tail_shape = p_blocks.shape[1:]
    row_panel = collect(p_blocks, "col", 0)
    column_rows = lax.all_gather(p_blocks, "row", axis=0, tiled=True)
    grouped = column_rows.reshape((cols_total, fan_count, piece_rows) + tail_shape)
    regrouped = lax.all_to_all(grouped, "col", split_axis=0, concat_axis=2, tiled=True)
    column_panel = regrouped.reshape((fan_count * cols_total * piece_rows,) + tail_shape)
    slot_count = KS_DEV * cols_total
    running = owner_terms(
        a_blocks[0, 0],
        a_rows[0, 0],
        a_cols[0, 0],
        coarse_slot[0, 0],
        row_panel,
        column_panel,
        slot_count,
    )
    reduced = sum_at_owner(running, "col", 0)
    return reduced.astype(jnp.bfloat16)[None]


def solution(mesh):
    placed = (
        P("row", "col", None, None, None),
        P("row", "col", None),
        P("row", "col", None),
        P(("row", "col"), None, None),
        P("row", "col", None, None, None),
    )
    return jax.shard_map(
        on_device, mesh=mesh, in_specs=placed, out_specs=P("row", "col", None), check_vma=False
    )
```

profile of v0, /device:TPU:32, one launch (start us, length us, event | category | flops | bytes accessed | tf_op | source)
XLA Modules:
  0.0 480.8 jit_solution(17363315479896694393)
XLA Ops:
  7.3 80.4 %all-gather.2.cloned.1.call-done = bf16[64,128,256]{2,1,0:T(8,128)(2,1)} async-done(((bf16[2,128,256]{2,1,0:T(8,128)(2,1)}), bf16[64,128,256]{2,1,0:T(8,128)(2,1)}) %all-gather.2.cloned.1.call-update) | async-done | bytes 4194320 | tf_op jit(solution)/shard_map/all_gather | solution.py:82
  87.7 58.3 %all_to_all.25 = bf16[16,2,2,128,256]{4,3,2,1,0:T(8,128)(2,1)} all-to-all(bf16[16,2,2,128,256]{4,3,2,1,0:T(8,128)(2,1)} %bitcast.70), channel_id=1, replica_groups=mesh['row'=32,'col'=16] {'col'}, dimensions={0} | all-to-all | bytes 8388608 | tf_op jit(solution)/shard_map/all_to_all | solution.py:84
  147.5 3.7 all-to-all-start.1
  153.5 4.6 copy.25
  158.1 23.2 %all-to-all-done.1 = bf16[16,2,128,256]{3,2,1,0:T(8,128)(2,1)S(1)} async-done(((bf16[16,2,128,256]{3,2,1,0:T(8,128)(2,1)}), bf16[16,2,128,256]{3,2,1,0:T(8,128)(2,1)S(1)}, u32[]{:S(2)}, u32[]{:S(2)}) %all-to-all-start.1) | async-done | bytes 2097184 | tf_op jit(solution)/shard_map/all_to_all | solution.py:11
  182.8 257.3 %while.10 = (s32[]{:T(128)}, f32[128,4096]{1,0:T(8,128)S(1)}, s32[6,16,4,4]{3,2,1,0:T(4,128)S(1)}, bf16[6,16,128,128]{3,2,1,0:T(8,128)(2,1)}, s32[6,16]{1,0:T(8,...) while((s32[]{:T(128)}, f32[128,4096]{1,0:T(8,128)S(1)}, ...), condition=%wide.region_2.3_spmd, body=%wide.region_0.2_spmd.sunk | while | flops 405277728 | bytes 46678312 | solution.py:71
  182.9 2.8 gather_fusion
  185.7 2.5 convolution_convert_fusion.2
  188.2 2.3 copy.33
  194.0 6.1 %convolution_bitcast_fusion.2 = f32[16,4,4,64,64]{3,4,1,2,0:T(8,128)} fusion(bf16[16,128,4,64,1]{1,3,4,2,0:T(8,128)(2,1)} %bitcast.66, bf16[16,128,4,64]{1,3,2,0:T(8,128)(2,1)} %bitcast.67, pred[16]{0:T(512)(128)(4,1)S(1)} %get-tuple-element.156), kind=kOutput, calls=%fused_computation.3.clone.1 | convolution fusion | flops 268959744 | bytes 6291472 | tf_op jit(solution)/shard_map/while/body/eval_jaxpr/knta,knsb->ktsab/dot_general | solution.py:57
  200.1 9.3 %copy.35 = f32[16,4,4,64,64]{4,3,2,1,0:T(8,128)} copy(f32[16,4,4,64,64]{3,4,1,2,0:T(8,128)} %convolution_bitcast_fusion.2) | data formatting | bytes 8388608 | tf_op jit(solution)/shard_map/while/body/eval_jaxpr/knta,knsb->ktsab/transpose | solution.py:57
  209.4 7.9 %reshape.191 = f32[256,4096]{1,0:T(8,128)} reshape(f32[16,4,4,64,64]{4,3,2,1,0:T(8,128)} %copy.35) | data formatting | bytes 8388608 | tf_op jit(solution)/shard_map/while/body/eval_jaxpr/reshape | solution.py:60
  217.4 8.3 %scatter_fusion = f32[128,4096]{1,0:T(8,128)S(1)} fusion(f32[128,4096]{1,0:T(8,128)S(1)} %get-tuple-element.167, s32[256]{0:T(256)S(1)} %bitcast.73, f32[256,4096]{1,0:T(8,128)} %reshape.191), kind=kCustom, calls=%fused_computation.2.clone.1 | custom fusion | flops 1048576 | bytes 12583936 | tf_op jit(solution)/shard_map/while/body/eval_jaxpr/scatter-add | solution.py:61
  225.7 2.8 gather_fusion
  228.6 2.5 convolution_convert_fusion.2
  231.1 2.3 copy.33
  236.9 6.1 %convolution_bitcast_fusion.2 = f32[16,4,4,64,64]{3,4,1,2,0:T(8,128)} fusion(bf16[16,128,4,64,1]{1,3,4,2,0:T(8,128)(2,1)} %bitcast.66, bf16[16,128,4,64]{1,3,2,0:T(8,128)(2,1)} %bitcast.67, pred[16]{0:T(512)(128)(4,1)S(1)} %get-tuple-element.156), kind=kOutput, calls=%fused_computation.3.clone.1 | convolution fusion | flops 268959744 | bytes 6291472 | tf_op jit(solution)/shard_map/while/body/eval_jaxpr/knta,knsb->ktsab/dot_general | solution.py:57
  243.0 9.3 %copy.35 = f32[16,4,4,64,64]{4,3,2,1,0:T(8,128)} copy(f32[16,4,4,64,64]{3,4,1,2,0:T(8,128)} %convolution_bitcast_fusion.2) | data formatting | bytes 8388608 | tf_op jit(solution)/shard_map/while/body/eval_jaxpr/knta,knsb->ktsab/transpose | solution.py:57
  252.3 7.9 %reshape.191 = f32[256,4096]{1,0:T(8,128)} reshape(f32[16,4,4,64,64]{4,3,2,1,0:T(8,128)} %copy.35) | data formatting | bytes 8388608 | tf_op jit(solution)/shard_map/while/body/eval_jaxpr/reshape | solution.py:60
  260.3 8.3 %scatter_fusion = f32[128,4096]{1,0:T(8,128)S(1)} fusion(f32[128,4096]{1,0:T(8,128)S(1)} %get-tuple-element.167, s32[256]{0:T(256)S(1)} %bitcast.73, f32[256,4096]{1,0:T(8,128)} %reshape.191), kind=kCustom, calls=%fused_computation.2.clone.1 | custom fusion | flops 1048576 | bytes 12583936 | tf_op jit(solution)/shard_map/while/body/eval_jaxpr/scatter-add | solution.py:61
  268.6 2.8 gather_fusion
  271.5 2.5 convolution_convert_fusion.2
  279.8 6.1 %convolution_bitcast_fusion.2 = f32[16,4,4,64,64]{3,4,1,2,0:T(8,128)} fusion(bf16[16,128,4,64,1]{1,3,4,2,0:T(8,128)(2,1)} %bitcast.66, bf16[16,128,4,64]{1,3,2,0:T(8,128)(2,1)} %bitcast.67, pred[16]{0:T(512)(128)(4,1)S(1)} %get-tuple-element.156), kind=kOutput, calls=%fused_computation.3.clone.1 | convolution fusion | flops 268959744 | bytes 6291472 | tf_op jit(solution)/shard_map/while/body/eval_jaxpr/knta,knsb->ktsab/dot_general | solution.py:57
  285.9 9.3 %copy.35 = f32[16,4,4,64,64]{4,3,2,1,0:T(8,128)} copy(f32[16,4,4,64,64]{3,4,1,2,0:T(8,128)} %convolution_bitcast_fusion.2) | data formatting | bytes 8388608 | tf_op jit(solution)/shard_map/while/body/eval_jaxpr/knta,knsb->ktsab/transpose | solution.py:57
  295.2 7.9 %reshape.191 = f32[256,4096]{1,0:T(8,128)} reshape(f32[16,4,4,64,64]{4,3,2,1,0:T(8,128)} %copy.35) | data formatting | bytes 8388608 | tf_op jit(solution)/shard_map/while/body/eval_jaxpr/reshape | solution.py:60
  303.2 8.3 %scatter_fusion = f32[128,4096]{1,0:T(8,128)S(1)} fusion(f32[128,4096]{1,0:T(8,128)S(1)} %get-tuple-element.167, s32[256]{0:T(256)S(1)} %bitcast.73, f32[256,4096]{1,0:T(8,128)} %reshape.191), kind=kCustom, calls=%fused_computation.2.clone.1 | custom fusion | flops 1048576 | bytes 12583936 | tf_op jit(solution)/shard_map/while/body/eval_jaxpr/scatter-add | solution.py:61
  311.5 2.8 gather_fusion
  314.3 2.5 convolution_convert_fusion.2
  316.9 2.3 copy.33
  322.7 6.1 %convolution_bitcast_fusion.2 = f32[16,4,4,64,64]{3,4,1,2,0:T(8,128)} fusion(bf16[16,128,4,64,1]{1,3,4,2,0:T(8,128)(2,1)} %bitcast.66, bf16[16,128,4,64]{1,3,2,0:T(8,128)(2,1)} %bitcast.67, pred[16]{0:T(512)(128)(4,1)S(1)} %get-tuple-element.156), kind=kOutput, calls=%fused_computation.3.clone.1 | convolution fusion | flops 268959744 | bytes 6291472 | tf_op jit(solution)/shard_map/while/body/eval_jaxpr/knta,knsb->ktsab/dot_general | solution.py:57
  328.8 9.3 %copy.35 = f32[16,4,4,64,64]{4,3,2,1,0:T(8,128)} copy(f32[16,4,4,64,64]{3,4,1,2,0:T(8,128)} %convolution_bitcast_fusion.2) | data formatting | bytes 8388608 | tf_op jit(solution)/shard_map/while/body/eval_jaxpr/knta,knsb->ktsab/transpose | solution.py:57
  338.0 7.9 %reshape.191 = f32[256,4096]{1,0:T(8,128)} reshape(f32[16,4,4,64,64]{4,3,2,1,0:T(8,128)} %copy.35) | data formatting | bytes 8388608 | tf_op jit(solution)/shard_map/while/body/eval_jaxpr/reshape | solution.py:60
  346.1 8.3 %scatter_fusion = f32[128,4096]{1,0:T(8,128)S(1)} fusion(f32[128,4096]{1,0:T(8,128)S(1)} %get-tuple-element.167, s32[256]{0:T(256)S(1)} %bitcast.73, f32[256,4096]{1,0:T(8,128)} %reshape.191), kind=kCustom, calls=%fused_computation.2.clone.1 | custom fusion | flops 1048576 | bytes 12583936 | tf_op jit(solution)/shard_map/while/body/eval_jaxpr/scatter-add | solution.py:61
  354.4 2.8 gather_fusion
  357.2 2.5 convolution_convert_fusion.2
  365.6 6.1 %convolution_bitcast_fusion.2 = f32[16,4,4,64,64]{3,4,1,2,0:T(8,128)} fusion(bf16[16,128,4,64,1]{1,3,4,2,0:T(8,128)(2,1)} %bitcast.66, bf16[16,128,4,64]{1,3,2,0:T(8,128)(2,1)} %bitcast.67, pred[16]{0:T(512)(128)(4,1)S(1)} %get-tuple-element.156), kind=kOutput, calls=%fused_computation.3.clone.1 | convolution fusion | flops 268959744 | bytes 6291472 | tf_op jit(solution)/shard_map/while/body/eval_jaxpr/knta,knsb->ktsab/dot_general | solution.py:57
  371.7 9.3 %copy.35 = f32[16,4,4,64,64]{4,3,2,1,0:T(8,128)} copy(f32[16,4,4,64,64]{3,4,1,2,0:T(8,128)} %convolution_bitcast_fusion.2) | data formatting | bytes 8388608 | tf_op jit(solution)/shard_map/while/body/eval_jaxpr/knta,knsb->ktsab/transpose | solution.py:57
  380.9 7.9 %reshape.191 = f32[256,4096]{1,0:T(8,128)} reshape(f32[16,4,4,64,64]{4,3,2,1,0:T(8,128)} %copy.35) | data formatting | bytes 8388608 | tf_op jit(solution)/shard_map/while/body/eval_jaxpr/reshape | solution.py:60
  389.0 8.3 %scatter_fusion = f32[128,4096]{1,0:T(8,128)S(1)} fusion(f32[128,4096]{1,0:T(8,128)S(1)} %get-tuple-element.167, s32[256]{0:T(256)S(1)} %bitcast.73, f32[256,4096]{1,0:T(8,128)} %reshape.191), kind=kCustom, calls=%fused_computation.2.clone.1 | custom fusion | flops 1048576 | bytes 12583936 | tf_op jit(solution)/shard_map/while/body/eval_jaxpr/scatter-add | solution.py:61
  397.3 2.8 gather_fusion
  400.1 2.5 convolution_convert_fusion.2
  402.6 2.3 copy.33
  408.5 6.1 %convolution_bitcast_fusion.2 = f32[16,4,4,64,64]{3,4,1,2,0:T(8,128)} fusion(bf16[16,128,4,64,1]{1,3,4,2,0:T(8,128)(2,1)} %bitcast.66, bf16[16,128,4,64]{1,3,2,0:T(8,128)(2,1)} %bitcast.67, pred[16]{0:T(512)(128)(4,1)S(1)} %get-tuple-element.156), kind=kOutput, calls=%fused_computation.3.clone.1 | convolution fusion | flops 268959744 | bytes 6291472 | tf_op jit(solution)/shard_map/while/body/eval_jaxpr/knta,knsb->ktsab/dot_general | solution.py:57
  414.6 9.3 %copy.35 = f32[16,4,4,64,64]{4,3,2,1,0:T(8,128)} copy(f32[16,4,4,64,64]{3,4,1,2,0:T(8,128)} %convolution_bitcast_fusion.2) | data formatting | bytes 8388608 | tf_op jit(solution)/shard_map/while/body/eval_jaxpr/knta,knsb->ktsab/transpose | solution.py:57
  423.8 7.9 %reshape.191 = f32[256,4096]{1,0:T(8,128)} reshape(f32[16,4,4,64,64]{4,3,2,1,0:T(8,128)} %copy.35) | data formatting | bytes 8388608 | tf_op jit(solution)/shard_map/while/body/eval_jaxpr/reshape | solution.py:60
  431.8 8.3 %scatter_fusion = f32[128,4096]{1,0:T(8,128)S(1)} fusion(f32[128,4096]{1,0:T(8,128)S(1)} %get-tuple-element.167, s32[256]{0:T(256)S(1)} %bitcast.73, f32[256,4096]{1,0:T(8,128)} %reshape.191), kind=kCustom, calls=%fused_computation.2.clone.1 | custom fusion | flops 1048576 | bytes 12583936 | tf_op jit(solution)/shard_map/while/body/eval_jaxpr/scatter-add | solution.py:61
  440.1 31.4 %all_to_all.26 = f32[16,8,4096]{2,1,0:T(8,128)} all-to-all(f32[16,8,4096]{2,1,0:T(8,128)S(1)} %bitcast.65), channel_id=1, replica_groups=mesh['row'=32,'col'=16] {'col'}, dimensions={0} | all-to-all | bytes 4194304 | tf_op jit(solution)/shard_map/all_to_all | solution.py:35
  471.6 2.3 reduce_sum.9
  (76 shorter events, 32.5 us)
Async XLA Ops:
  6.5 81.2 %all-gather.2.cloned.1.call-start = ((), (), s32[]{:S(2)}) async-start(), calls=%async_computation.3 | async-start | bytes 4325376 | tf_op jit(solution)/shard_map/all_gather | solution.py:82
  87.7 58.3 %copy-start.1 = (bf16[2,128,256]{2,1,0:T(8,128)(2,1)S(1)}, bf16[2,128,256]{2,1,0:T(8,128)(2,1)}, u32[]{:S(2)}) copy-start(bf16[2,128,256]{2,1,0:T(8,128)(2,1)} %param.10) | copy-start | bytes 393220
  146.0 5.9 %copy-start.3 = (s32[1,1,96]{2,1,0:T(1,128)S(1)}, s32[1,1,96]{2,1,0:T(1,128)}, u32[]{:S(2)}) copy-start(s32[1,1,96]{2,1,0:T(1,128)} %param.9) | copy-start | bytes 1156
  146.0 6.6 %copy-start.4 = (s32[1,1,96]{2,1,0:T(1,128)S(1)}, s32[1,1,96]{2,1,0:T(1,128)}, u32[]{:S(2)}) copy-start(s32[1,1,96]{2,1,0:T(1,128)} %param.8) | copy-start | bytes 1156
  146.0 7.3 %copy-start.2 = (s32[1,1,96,4,4]{2,4,3,1,0:T(4,128)S(1)}, s32[1,1,96,4,4]{2,4,3,1,0:T(4,128)}, u32[]{:S(2)}) copy-start(s32[1,1,96,4,4]{2,4,3,1,0:T(4,128)} %param.11) | copy-start | bytes 18436
  147.5 33.7 %all-to-all-start.1 = ((bf16[16,2,128,256]{3,2,1,0:T(8,128)(2,1)}), bf16[16,2,128,256]{3,2,1,0:T(8,128)(2,1)S(1)}, u32[]{:S(2)}, u32[]{:S(2)}) async-start(bf16[16,2,128,256]{3,2,1,0:T(8,128)(2,1)} %broadcast_in_dim.32), calls=%async_computation.1 | async-start | bytes 4194304 | tf_op jit(solution)/shard_map/all_to_all | solution.py:11
  181.3 1.3 copy-start
Sparse Core Ops, SparseCore 0:
  9.5 78.1 all-gather.1
where the time goes:
time: 483 us; the launch traced here: 481 us
  local copies, waits for them, and re-layouts  164 us (34%)
  waiting for transfers between devices  104 us (22%)
  blocking collectives  89.7 us (19%)
  other arithmetic  53.6 us (11%)
  matrix products  51.7 us (11%)
  between operations  13.4 us (3%)
    all_gather x1, waiting for transfers between devices, on_device(): column_rows = lax.all_gather(p_blocks, 'row', axis=0, tiled=True)  80.4 us
    all_to_all x1, blocking collectives, on_device(): lax.all_to_all(grouped, 'col', split_axis=0, concat_axis=2, tiled=True)  58.3 us
    transpose x6, local copies, waits for them, and re-layouts, accumulate(): jnp.einsum('knta,knsb->ktsab', left_split, right_split, preferred_element...  55.5 us
    scatter-add x6, other arithmetic, accumulate(): running = running.at[sls.reshape(-1)].add(contribs)  49.7 us
    reshape x6, local copies, waits for them, and re-layouts, accumulate(): contribs.reshape(group_size * agg_blocks * agg_blocks, agg_width * agg_wi...  47.4 us
    dot_general x6, matrix products, accumulate(): jnp.einsum('knta,knsb->ktsab', left_split, right_split, preferred_element...  36.6 us
    all_to_all x1, blocking collectives, sum_at_owner(): lax.all_to_all(tiles, axis, split_axis=0, concat_axis=0, tiled=True)  31.4 us
    all_to_all x1, waiting for transfers between devices, copy_for_each(): lax.all_to_all(jnp.broadcast_to(array[None], (size, *array.shape)), axis,...  23.2 us
  transfers between devices with their start and end apart: 2, of which 2 were waited for; matrix products, arithmetic and copies ran while one was open for 1% of the time, Pallas kernels for 0%

commit v1 on v0

--- a/solution.py
+++ b/solution.py
@@ -79,7 +79,9 @@
     piece_rows = p_blocks.shape[0]
     tail_shape = p_blocks.shape[1:]
     row_panel = collect(p_blocks, "col", 0)
-    column_rows = lax.all_gather(p_blocks, "row", axis=0, tiled=True)
+    column_rows = jnp.concatenate(
+        lax.all_to_all(jnp.stack([p_blocks] * lax.axis_size("row")), "row", 0, 0), axis=0
+    )
     grouped = column_rows.reshape((cols_total, fan_count, piece_rows) + tail_shape)
     regrouped = lax.all_to_all(grouped, "col", split_axis=0, concat_axis=2, tiled=True)
     column_panel = regrouped.reshape((fan_count * cols_total * piece_rows,) + tail_shape)

time: 483 us -> 597 us (1.24)
  the two profiles are of different devices: /device:TPU:32 before, /device:TPU:64 now
where the time goes in v1:
time: 597 us; the launch traced here: 595 us
  blocking collectives  293 us (49%)
  local copies, waits for them, and re-layouts  165 us (28%)
  other arithmetic  53.5 us (9%)
  matrix products  51.8 us (9%)
  waiting for transfers between devices  26.1 us (4%)
    all_to_all x1, blocking collectives, on_device(): lax.all_to_all(jnp.stack([p_blocks] * lax.axis_size('row')), 'row', 0, 0)  201 us
    all_to_all x1, blocking collectives, on_device(): lax.all_to_all(grouped, 'col', split_axis=0, concat_axis=2, tiled=True)  60.6 us
    transpose x6, local copies, waits for them, and re-layouts, accumulate(): jnp.einsum('knta,knsb->ktsab', left_split, right_split, preferred_element...  55.6 us
    scatter-add x6, other arithmetic, accumulate(): running = running.at[sls.reshape(-1)].add(contribs)  49.7 us
    reshape x6, local copies, waits for them, and re-layouts, accumulate(): contribs.reshape(group_size * agg_blocks * agg_blocks, agg_width * agg_wi...  47.4 us
    dot_general x6, matrix products, accumulate(): jnp.einsum('knta,knsb->ktsab', left_split, right_split, preferred_element...  36.6 us
    all_to_all x1, blocking collectives, sum_at_owner(): lax.all_to_all(tiles, axis, split_axis=0, concat_axis=0, tiled=True)  31.3 us
    all_to_all x1, waiting for transfers between devices, copy_for_each(): lax.all_to_all(jnp.broadcast_to(array[None], (size, *array.shape)), axis,...  26.1 us
  transfers between devices with their start and end apart: 1, of which 1 were waited for; matrix products, arithmetic and copies ran while one was open for 1% of the time, Pallas kernels for 0%

profile of v1, /device:TPU:64, one launch (start us, length us, event | category | flops | bytes accessed | tf_op | source)
XLA Modules:
  0.0 594.6 jit_solution(9948372429511865811)
XLA Ops:
  1.4 201.2 %all_to_all.30 = bf16[32,2,128,256]{3,2,1,0:T(8,128)(2,1)S(1)} all-to-all(bf16[32,2,128,256]{3,2,1,0:T(8,128)(2,1)S(1)} %stack.2), channel_id=1, replica_groups=mesh['row'=32,'col'=16] {'row'}, dimensions={0} | all-to-all | bytes 8388608 | tf_op jit(solution)/shard_map/all_to_all | solution.py:83
  202.6 60.6 %all_to_all.31 = bf16[16,2,2,128,256]{4,3,2,1,0:T(8,128)(2,1)} all-to-all(bf16[16,2,2,128,256]{4,3,2,1,0:T(8,128)(2,1)S(1)} %bitcast.70), channel_id=1, replica_groups=mesh['row'=32,'col'=16] {'col'}, dimensions={0} | all-to-all | bytes 8388608 | tf_op jit(solution)/shard_map/all_to_all | solution.py:86
  264.8 4.1 all-to-all-start.2
  270.9 4.6 copy.14
  275.6 26.1 %all-to-all-done.2 = bf16[16,2,128,256]{3,2,1,0:T(8,128)(2,1)S(1)} async-done(((bf16[16,2,128,256]{3,2,1,0:T(8,128)(2,1)}), bf16[16,2,128,256]{3,2,1,0:T(8,128)(2,1)S(1)}, u32[]{:S(2)}, u32[]{:S(2)}) %all-to-all-start.2) | async-done | bytes 2097184 | tf_op jit(solution)/shard_map/all_to_all | solution.py:11
  303.2 257.7 %while.10 = (s32[]{:T(128)}, f32[128,4096]{1,0:T(8,128)S(1)}, s32[6,16,4,4]{3,2,1,0:T(4,128)S(1)}, bf16[6,16,128,128]{3,2,1,0:T(8,128)(2,1)}, s32[6,16]{1,0:T(8,...) while((s32[]{:T(128)}, f32[128,4096]{1,0:T(8,128)S(1)}, ...), condition=%wide.region_2.3_spmd, body=%wide.region_0.2_spmd.sunk | while | flops 405277728 | bytes 46678312 | solution.py:71
  303.2 2.8 gather_fusion
  306.1 2.5 convolution_convert_fusion.2
  308.6 2.3 copy.22
  314.5 6.1 %convolution_bitcast_fusion.2 = f32[16,4,4,64,64]{3,4,1,2,0:T(8,128)} fusion(bf16[16,128,4,64,1]{1,3,4,2,0:T(8,128)(2,1)} %bitcast.65, bf16[16,128,4,64]{1,3,2,0:T(8,128)(2,1)} %bitcast.66, pred[16]{0:T(512)(128)(4,1)S(1)} %get-tuple-element.140), kind=kOutput, calls=%fused_computation.3.clone.1 | convolution fusion | flops 268959744 | bytes 6291472 | tf_op jit(solution)/shard_map/while/body/eval_jaxpr/knta,knsb->ktsab/dot_general | solution.py:57
  320.6 9.3 %copy.24 = f32[16,4,4,64,64]{4,3,2,1,0:T(8,128)} copy(f32[16,4,4,64,64]{3,4,1,2,0:T(8,128)} %convolution_bitcast_fusion.2) | data formatting | bytes 8388608 | tf_op jit(solution)/shard_map/while/body/eval_jaxpr/knta,knsb->ktsab/transpose | solution.py:57
  329.8 7.9 %reshape.189 = f32[256,4096]{1,0:T(8,128)} reshape(f32[16,4,4,64,64]{4,3,2,1,0:T(8,128)} %copy.24) | data formatting | bytes 8388608 | tf_op jit(solution)/shard_map/while/body/eval_jaxpr/reshape | solution.py:60
  337.9 8.3 %scatter_fusion = f32[128,4096]{1,0:T(8,128)S(1)} fusion(f32[128,4096]{1,0:T(8,128)S(1)} %get-tuple-element.151, s32[256]{0:T(256)S(1)} %bitcast.73, f32[256,4096]{1,0:T(8,128)} %reshape.189), kind=kCustom, calls=%fused_computation.2.clone.1 | custom fusion | flops 1048576 | bytes 12583936 | tf_op jit(solution)/shard_map/while/body/eval_jaxpr/scatter-add | solution.py:61
  346.2 2.8 gather_fusion
  349.0 2.5 convolution_convert_fusion.2
  351.6 2.3 copy.22
  357.4 6.1 %convolution_bitcast_fusion.2 = f32[16,4,4,64,64]{3,4,1,2,0:T(8,128)} fusion(bf16[16,128,4,64,1]{1,3,4,2,0:T(8,128)(2,1)} %bitcast.65, bf16[16,128,4,64]{1,3,2,0:T(8,128)(2,1)} %bitcast.66, pred[16]{0:T(512)(128)(4,1)S(1)} %get-tuple-element.140), kind=kOutput, calls=%fused_computation.3.clone.1 | convolution fusion | flops 268959744 | bytes 6291472 | tf_op jit(solution)/shard_map/while/body/eval_jaxpr/knta,knsb->ktsab/dot_general | solution.py:57
  363.5 9.3 %copy.24 = f32[16,4,4,64,64]{4,3,2,1,0:T(8,128)} copy(f32[16,4,4,64,64]{3,4,1,2,0:T(8,128)} %convolution_bitcast_fusion.2) | data formatting | bytes 8388608 | tf_op jit(solution)/shard_map/while/body/eval_jaxpr/knta,knsb->ktsab/transpose | solution.py:57
  372.8 7.9 %reshape.189 = f32[256,4096]{1,0:T(8,128)} reshape(f32[16,4,4,64,64]{4,3,2,1,0:T(8,128)} %copy.24) | data formatting | bytes 8388608 | tf_op jit(solution)/shard_map/while/body/eval_jaxpr/reshape | solution.py:60
  380.8 8.3 %scatter_fusion = f32[128,4096]{1,0:T(8,128)S(1)} fusion(f32[128,4096]{1,0:T(8,128)S(1)} %get-tuple-element.151, s32[256]{0:T(256)S(1)} %bitcast.73, f32[256,4096]{1,0:T(8,128)} %reshape.189), kind=kCustom, calls=%fused_computation.2.clone.1 | custom fusion | flops 1048576 | bytes 12583936 | tf_op jit(solution)/shard_map/while/body/eval_jaxpr/scatter-add | solution.py:61
  389.1 2.8 gather_fusion
  392.0 2.5 convolution_convert_fusion.2
  394.5 2.3 copy.22
  400.4 6.1 %convolution_bitcast_fusion.2 = f32[16,4,4,64,64]{3,4,1,2,0:T(8,128)} fusion(bf16[16,128,4,64,1]{1,3,4,2,0:T(8,128)(2,1)} %bitcast.65, bf16[16,128,4,64]{1,3,2,0:T(8,128)(2,1)} %bitcast.66, pred[16]{0:T(512)(128)(4,1)S(1)} %get-tuple-element.140), kind=kOutput, calls=%fused_computation.3.clone.1 | convolution fusion | flops 268959744 | bytes 6291472 | tf_op jit(solution)/shard_map/while/body/eval_jaxpr/knta,knsb->ktsab/dot_general | solution.py:57
  406.5 9.3 %copy.24 = f32[16,4,4,64,64]{4,3,2,1,0:T(8,128)} copy(f32[16,4,4,64,64]{3,4,1,2,0:T(8,128)} %convolution_bitcast_fusion.2) | data formatting | bytes 8388608 | tf_op jit(solution)/shard_map/while/body/eval_jaxpr/knta,knsb->ktsab/transpose | solution.py:57
  415.7 7.9 %reshape.189 = f32[256,4096]{1,0:T(8,128)} reshape(f32[16,4,4,64,64]{4,3,2,1,0:T(8,128)} %copy.24) | data formatting | bytes 8388608 | tf_op jit(solution)/shard_map/while/body/eval_jaxpr/reshape | solution.py:60
  423.8 8.3 %scatter_fusion = f32[128,4096]{1,0:T(8,128)S(1)} fusion(f32[128,4096]{1,0:T(8,128)S(1)} %get-tuple-element.151, s32[256]{0:T(256)S(1)} %bitcast.73, f32[256,4096]{1,0:T(8,128)} %reshape.189), kind=kCustom, calls=%fused_computation.2.clone.1 | custom fusion | flops 1048576 | bytes 12583936 | tf_op jit(solution)/shard_map/while/body/eval_jaxpr/scatter-add | solution.py:61
  432.1 2.8 gather_fusion
  434.9 2.5 convolution_convert_fusion.2
  437.4 2.3 copy.22
  443.3 6.1 %convolution_bitcast_fusion.2 = f32[16,4,4,64,64]{3,4,1,2,0:T(8,128)} fusion(bf16[16,128,4,64,1]{1,3,4,2,0:T(8,128)(2,1)} %bitcast.65, bf16[16,128,4,64]{1,3,2,0:T(8,128)(2,1)} %bitcast.66, pred[16]{0:T(512)(128)(4,1)S(1)} %get-tuple-element.140), kind=kOutput, calls=%fused_computation.3.clone.1 | convolution fusion | flops 268959744 | bytes 6291472 | tf_op jit(solution)/shard_map/while/body/eval_jaxpr/knta,knsb->ktsab/dot_general | solution.py:57
  449.4 9.3 %copy.24 = f32[16,4,4,64,64]{4,3,2,1,0:T(8,128)} copy(f32[16,4,4,64,64]{3,4,1,2,0:T(8,128)} %convolution_bitcast_fusion.2) | data formatting | bytes 8388608 | tf_op jit(solution)/shard_map/while/body/eval_jaxpr/knta,knsb->ktsab/transpose | solution.py:57
  458.7 7.9 %reshape.189 = f32[256,4096]{1,0:T(8,128)} reshape(f32[16,4,4,64,64]{4,3,2,1,0:T(8,128)} %copy.24) | data formatting | bytes 8388608 | tf_op jit(solution)/shard_map/while/body/eval_jaxpr/reshape | solution.py:60
  466.7 8.3 %scatter_fusion = f32[128,4096]{1,0:T(8,128)S(1)} fusion(f32[128,4096]{1,0:T(8,128)S(1)} %get-tuple-element.151, s32[256]{0:T(256)S(1)} %bitcast.73, f32[256,4096]{1,0:T(8,128)} %reshape.189), kind=kCustom, calls=%fused_computation.2.clone.1 | custom fusion | flops 1048576 | bytes 12583936 | tf_op jit(solution)/shard_map/while/body/eval_jaxpr/scatter-add | solution.py:61
  475.0 2.8 gather_fusion
  477.9 2.5 convolution_convert_fusion.2
  486.3 6.1 %convolution_bitcast_fusion.2 = f32[16,4,4,64,64]{3,4,1,2,0:T(8,128)} fusion(bf16[16,128,4,64,1]{1,3,4,2,0:T(8,128)(2,1)} %bitcast.65, bf16[16,128,4,64]{1,3,2,0:T(8,128)(2,1)} %bitcast.66, pred[16]{0:T(512)(128)(4,1)S(1)} %get-tuple-element.140), kind=kOutput, calls=%fused_computation.3.clone.1 | convolution fusion | flops 268959744 | bytes 6291472 | tf_op jit(solution)/shard_map/while/body/eval_jaxpr/knta,knsb->ktsab/dot_general | solution.py:57
  492.4 9.3 %copy.24 = f32[16,4,4,64,64]{4,3,2,1,0:T(8,128)} copy(f32[16,4,4,64,64]{3,4,1,2,0:T(8,128)} %convolution_bitcast_fusion.2) | data formatting | bytes 8388608 | tf_op jit(solution)/shard_map/while/body/eval_jaxpr/knta,knsb->ktsab/transpose | solution.py:57
  501.6 7.9 %reshape.189 = f32[256,4096]{1,0:T(8,128)} reshape(f32[16,4,4,64,64]{4,3,2,1,0:T(8,128)} %copy.24) | data formatting | bytes 8388608 | tf_op jit(solution)/shard_map/while/body/eval_jaxpr/reshape | solution.py:60
  509.6 8.3 %scatter_fusion = f32[128,4096]{1,0:T(8,128)S(1)} fusion(f32[128,4096]{1,0:T(8,128)S(1)} %get-tuple-element.151, s32[256]{0:T(256)S(1)} %bitcast.73, f32[256,4096]{1,0:T(8,128)} %reshape.189), kind=kCustom, calls=%fused_computation.2.clone.1 | custom fusion | flops 1048576 | bytes 12583936 | tf_op jit(solution)/shard_map/while/body/eval_jaxpr/scatter-add | solution.py:61
  518.0 2.8 gather_fusion
  520.8 2.5 convolution_convert_fusion.2
  523.3 2.3 copy.22
  529.2 6.1 %convolution_bitcast_fusion.2 = f32[16,4,4,64,64]{3,4,1,2,0:T(8,128)} fusion(bf16[16,128,4,64,1]{1,3,4,2,0:T(8,128)(2,1)} %bitcast.65, bf16[16,128,4,64]{1,3,2,0:T(8,128)(2,1)} %bitcast.66, pred[16]{0:T(512)(128)(4,1)S(1)} %get-tuple-element.140), kind=kOutput, calls=%fused_computation.3.clone.1 | convolution fusion | flops 268959744 | bytes 6291472 | tf_op jit(solution)/shard_map/while/body/eval_jaxpr/knta,knsb->ktsab/dot_general | solution.py:57
  535.3 9.3 %copy.24 = f32[16,4,4,64,64]{4,3,2,1,0:T(8,128)} copy(f32[16,4,4,64,64]{3,4,1,2,0:T(8,128)} %convolution_bitcast_fusion.2) | data formatting | bytes 8388608 | tf_op jit(solution)/shard_map/while/body/eval_jaxpr/knta,knsb->ktsab/transpose | solution.py:57
  544.6 7.9 %reshape.189 = f32[256,4096]{1,0:T(8,128)} reshape(f32[16,4,4,64,64]{4,3,2,1,0:T(8,128)} %copy.24) | data formatting | bytes 8388608 | tf_op jit(solution)/shard_map/while/body/eval_jaxpr/reshape | solution.py:60
  552.6 8.3 %scatter_fusion = f32[128,4096]{1,0:T(8,128)S(1)} fusion(f32[128,4096]{1,0:T(8,128)S(1)} %get-tuple-element.151, s32[256]{0:T(256)S(1)} %bitcast.73, f32[256,4096]{1,0:T(8,128)} %reshape.189), kind=kCustom, calls=%fused_computation.2.clone.1 | custom fusion | flops 1048576 | bytes 12583936 | tf_op jit(solution)/shard_map/while/body/eval_jaxpr/scatter-add | solution.py:61
  560.9 31.3 %all_to_all.32 = f32[16,8,4096]{2,1,0:T(8,128)} all-to-all(f32[16,8,4096]{2,1,0:T(8,128)S(1)} %bitcast.64), channel_id=1, replica_groups=mesh['row'=32,'col'=16] {'col'}, dimensions={0} | all-to-all | bytes 4194304 | tf_op jit(solution)/shard_map/all_to_all | solution.py:35
  (75 shorter events, 33.2 us)
Async XLA Ops:
  202.6 60.6 %copy-start.1 = (bf16[2,128,256]{2,1,0:T(8,128)(2,1)S(1)}, bf16[2,128,256]{2,1,0:T(8,128)(2,1)}, u32[]{:S(2)}) copy-start(bf16[2,128,256]{2,1,0:T(8,128)(2,1)} %param.10) | copy-start | bytes 393220
  263.2 6.2 %copy-start.3 = (s32[1,1,96]{2,1,0:T(1,128)S(1)}, s32[1,1,96]{2,1,0:T(1,128)}, u32[]{:S(2)}) copy-start(s32[1,1,96]{2,1,0:T(1,128)} %param.9) | copy-start | bytes 1156
  263.2 6.9 %copy-start.4 = (s32[1,1,96]{2,1,0:T(1,128)S(1)}, s32[1,1,96]{2,1,0:T(1,128)}, u32[]{:S(2)}) copy-start(s32[1,1,96]{2,1,0:T(1,128)} %param.8) | copy-start | bytes 1156
  263.2 7.6 %copy-start.2 = (s32[1,1,96,4,4]{2,4,3,1,0:T(4,128)S(1)}, s32[1,1,96,4,4]{2,4,3,1,0:T(4,128)}, u32[]{:S(2)}) copy-start(s32[1,1,96,4,4]{2,4,3,1,0:T(4,128)} %param.11) | copy-start | bytes 18436
  264.8 36.9 %all-to-all-start.2 = ((bf16[16,2,128,256]{3,2,1,0:T(8,128)(2,1)}), bf16[16,2,128,256]{3,2,1,0:T(8,128)(2,1)S(1)}, u32[]{:S(2)}, u32[]{:S(2)}) async-start(bf16[16,2,128,256]{3,2,1,0:T(8,128)(2,1)} %broadcast_in_dim.32), calls=%async_computation.2 | async-start | bytes 4194304 | tf_op jit(solution)/shard_map/all_to_all | solution.py:11
  301.7 1.3 copy-start
